TPU v7x, 32 devices: a whole 2x2x4 slice. The times are simulated.
32 devices in a mesh: bins: 8 (over y, x, core), chan: 4 (over z).
Axes of the slice: x: 2, y: 2, z: 4, core: 2. Of those that a mesh axis runs over, the one named last changes fastest.
Arguments:
- samples: float32 [8, 512, 512], P('bins', 'chan'), may hold values from -18 to 18
- groups: int32 [512], replicated, may hold values from 0 to 63, never falling along the last dimension, each value on 1 to 16 neighbouring positions
- dm_delay: int32 [2048], replicated, may hold values from 0 to 4095
- widths: int32 [8], replicated, may hold values from 0 to 4, as said below
Outputs:
- whitened: float32 [8, 512, 2048], P(None, 'bins', 'chan')
Inputs may be any that keep to these rules, and one draw needn't show every extreme that they name: `groups`: group numbers never fall along the channels; each group holds 1 to 16 channels. `widths`: in every draw some band has half-width 4 and some band half-width 0.
All inputs are finite; a program needn't handle non-finite values.
Results may differ from a plain program's by a relative error of at most 0.0037.
Values may be sent and summed in bfloat16 or wider, within the bound.
A program may use at most 128 MiB of HBM per device.

v0:
```python
import math

import jax
import jax.numpy as jnp
from jax import lax
from jax.sharding import PartitionSpec as P

CHANNELS = 512
GROUPS = 64
BANDS = 8
HALF = 4


FLOOR_VALUE = 0.5


def with_halo(block, sides, width):
    for axis, dim in sides:
        count = lax.axis_size(axis)
        forward = [(i, i + 1) for i in range(count - 1)]
        forward.append((count - 1, 0))
        backward = [(target, source) for source, target in forward]
        low = lax.ppermute(
            lax.slice_in_dim(block, block.shape[dim] - width, None, axis=dim), axis, forward
        )
        high = lax.ppermute(lax.slice_in_dim(block, 0, width, axis=dim), axis, backward)
        block = jnp.concatenate([low, block, high], axis=dim)
    return block


def cycle_table(first_index, second_index, period):
    product = first_index[:, None] * second_index[None, :] % period
    phases = product.astype(jnp.float32) * (2.0 * math.pi / period)
    return (jnp.cos(phases), jnp.sin(phases))


def dedisperse(spectra, groups, delay_list, phase_index, total_bins, shard_bins):
    remain = GROUPS - groups
    sweep_scale = 2048 * remain * remain // (GROUPS * GROUPS)
    delays = sweep_scale[:, None] * delay_list[None, :] // 1024
    angle_step = 2.0 * math.pi / total_bins
    band_length = shard_bins * lax.axis_size("bins")

    def one_band(band):
        bin_index = (
            band * band_length + phase_index * shard_bins + jnp.arange(shard_bins, dtype=jnp.int32)
        )
        product = bin_index[:, None, None] * delays[None, :, :] % total_bins
        phases = product.astype(jnp.float32) * angle_step
        ramp_table = jnp.concatenate([jnp.cos(phases), jnp.sin(phases)], axis=1).astype(
            jnp.bfloat16
        )
        local_bins = spectra[band]
        real_row = jnp.concatenate([local_bins[:, 0], -local_bins[:, 1]], axis=1)
        imag_row = jnp.concatenate([local_bins[:, 1], local_bins[:, 0]], axis=1)
        operand = jnp.stack([real_row, imag_row], axis=1)
        return jnp.einsum("krc,kcm->krm", operand, ramp_table, preferred_element_type=jnp.float32)

    return lax.map(one_band, jnp.arange(BANDS, dtype=jnp.int32))


def shards(samples, groups, dm_delay, widths):
    highest = lax.Precision.HIGHEST
    phase_count = lax.axis_size("bins")
    phase_index = lax.axis_index("bins")
    chan_index = lax.axis_index("chan")
    length = samples.shape[2]
    shard_bins = length // phase_count
    total_bins = length * phase_count
    time_index = jnp.arange(length, dtype=jnp.int32)
    cos_first, sin_first = cycle_table(time_index, time_index, length)
    band_index = jnp.arange(BANDS, dtype=jnp.int32)
    source_index = jnp.arange(phase_count, dtype=jnp.int32)
    cos_second, sin_second = cycle_table(source_index, band_index, phase_count)
    scale_value = total_bins ** (-0.5)
    signal = samples[0]
    real_first = jnp.einsum("kb,cb->kc", cos_first, signal, precision=highest)
    imag_first = -jnp.einsum("kb,cb->kc", sin_first, signal, precision=highest)
    twist_cos, twist_sin = cycle_table(time_index, jnp.reshape(phase_index, (1,)), total_bins)
    turned_real = real_first * twist_cos + imag_first * twist_sin
    turned_imag = imag_first * twist_cos - real_first * twist_sin
    outgoing = jnp.stack([turned_real, turned_imag], axis=0)[None]
    received = lax.all_to_all(outgoing, "bins", split_axis=2, concat_axis=0, tiled=True)
    real_in = received[:, 0]
    imag_in = received[:, 1]
    real_out = jnp.einsum("arc,ak->krc", real_in, cos_second, precision=highest) + jnp.einsum(
        "arc,ak->krc", imag_in, sin_second, precision=highest
    )
    imag_out = jnp.einsum("arc,ak->krc", imag_in, cos_second, precision=highest) - jnp.einsum(
        "arc,ak->krc", real_in, sin_second, precision=highest
    )
    spectra = (jnp.stack([real_out, imag_out], axis=2) * scale_value).astype(jnp.bfloat16)
    local_channels = spectra.shape[3]
    local_groups = lax.dynamic_slice_in_dim(groups, chan_index * local_channels, local_channels)
    partial_terms = dedisperse(spectra, local_groups, dm_delay, phase_index, total_bins, shard_bins)
    summed = lax.psum_scatter(partial_terms, "chan", scatter_dimension=3, tiled=True)
    real_sum = summed[:, :, 0]
    imag_sum = summed[:, :, 1]
    powers = (real_sum * real_sum + imag_sum * imag_sum) / CHANNELS
    padded = with_halo(powers, (("bins", 1),), HALF)
    lower_rim = padded[:, :HALF]
    middle = padded[:, HALF : HALF + shard_bins]
    upper_rim = padded[:, HALF + shard_bins :]
    zero_rows = jnp.zeros_like(lower_rim[:1])
    lower_rim = jnp.where(
        phase_index == 0, jnp.concatenate([zero_rows, lower_rim[:-1]], axis=0), lower_rim
    )
    upper_rim = jnp.where(
        phase_index == phase_count - 1,
        jnp.concatenate([upper_rim[1:], zero_rows], axis=0),
        upper_rim,
    )
    extended = jnp.concatenate([lower_rim, middle, upper_rim], axis=1)
    row_bins = (
        band_index[:, None] * length
        + phase_index * shard_bins
        + jnp.arange(shard_bins, dtype=jnp.int32)[None, :]
    )
    half_width = widths[:, None]
    window_sum = jnp.zeros(powers.shape, jnp.float32)
    counted = jnp.zeros(row_bins.shape, jnp.float32)
    for offset in range(-HALF, HALF + 1):
        neighbour = row_bins + offset
        inside = (abs(offset) <= half_width) & (neighbour >= 0) & (neighbour < BANDS * length)
        weight = inside.astype(jnp.float32)
        window_sum = (
            window_sum
            + weight[:, :, None] * extended[:, HALF + offset : HALF + offset + shard_bins]
        )
        counted = counted + weight
    local_mean = window_sum / counted[:, :, None]
    return powers / jnp.maximum(local_mean, FLOOR_VALUE)


def solution(mesh):
    in_specs = (P("bins", "chan", None), P(), P(), P())
    out_specs = P(None, "bins", "chan")
    return jax.shard_map(shards, mesh=mesh, in_specs=in_specs, out_specs=out_specs, check_vma=False)
```

profile of v0, /device:TPU:0, one launch (start us, length us, event | category | flops | bytes accessed | tf_op | source)
XLA Modules:
  0.0 2573.3 jit_solution(16532895939982403912)
XLA Ops:
  6.5 0.9 copy-done
  7.5 4.8 convolution_negate_fusion
  12.3 4.8 add_bitcast_fusion
  17.2 1.2 copy.25
  18.4 5.2 all-to-all-start
  23.6 0.8 and_select_fusion
  24.4 8.9 all-to-all-done
  35.4 2375.1 %while.13 = (s32[]{:T(128)}, f32[8,64,2,2048]{3,1,0,2:T(8,128)}, s32[8]{0:T(128)S(1)}, bf16[8,64,2,128]{3,1,2,0:T(8,128)(2,1)S(1)}, s32[]{:T(128)}, /*index=5*/s...) while((s32[]{:T(128)}, f32[8,64,2,2048]{3,1,0,2:T(8,128)}, ...), condition=%wide.region_1.2_spmd.clone, body=%wide.region_0.1_spmd.clone.sunk | while | flops 541335616 | bytes 139945168 | solution.py:59
  35.6 1.4 add_select_fusion.6
  38.2 268.1 %cosine_convert_fusion.2 = (bf16[64,128,2048]{2,1,0:T(8,128)(2,1)}, bf16[64,128,2048]{2,1,0:T(8,128)(2,1)}) fusion(s32[128,2048]{1,0:T(8,128)S(1)} %add_select_fusion.6, s32[64]{0:T(128)S(1)} %iota_add_fusion.3), kind=kLoop, calls=%fused_computation.14.clone.1 | loop fusion | flops 268435456 | bytes 68157696 | tf_op jit(solution)/shard_map/convert
  308.4 22.4 fusion.176
  330.8 1.6 copy_dynamic-update-slice_fusion.2
  332.4 1.4 add_select_fusion.6
  335.0 268.1 %cosine_convert_fusion.2 = (bf16[64,128,2048]{2,1,0:T(8,128)(2,1)}, bf16[64,128,2048]{2,1,0:T(8,128)(2,1)}) fusion(s32[128,2048]{1,0:T(8,128)S(1)} %add_select_fusion.6, s32[64]{0:T(128)S(1)} %iota_add_fusion.3), kind=kLoop, calls=%fused_computation.14.clone.1 | loop fusion | flops 268435456 | bytes 68157696 | tf_op jit(solution)/shard_map/convert
  605.3 22.4 fusion.176
  627.7 1.6 copy_dynamic-update-slice_fusion.2
  629.3 1.4 add_select_fusion.6
  630.6 0.6 dynamic_slice.24
  631.9 268.1 %cosine_convert_fusion.2 = (bf16[64,128,2048]{2,1,0:T(8,128)(2,1)}, bf16[64,128,2048]{2,1,0:T(8,128)(2,1)}) fusion(s32[128,2048]{1,0:T(8,128)S(1)} %add_select_fusion.6, s32[64]{0:T(128)S(1)} %iota_add_fusion.3), kind=kLoop, calls=%fused_computation.14.clone.1 | loop fusion | flops 268435456 | bytes 68157696 | tf_op jit(solution)/shard_map/convert
  902.1 22.4 fusion.176
  924.5 1.6 copy_dynamic-update-slice_fusion.2
  926.1 1.4 add_select_fusion.6
  927.5 0.6 dynamic_slice.24
  928.8 268.1 %cosine_convert_fusion.2 = (bf16[64,128,2048]{2,1,0:T(8,128)(2,1)}, bf16[64,128,2048]{2,1,0:T(8,128)(2,1)}) fusion(s32[128,2048]{1,0:T(8,128)S(1)} %add_select_fusion.6, s32[64]{0:T(128)S(1)} %iota_add_fusion.3), kind=kLoop, calls=%fused_computation.14.clone.1 | loop fusion | flops 268435456 | bytes 68157696 | tf_op jit(solution)/shard_map/convert
  1199.0 22.4 fusion.176
  1221.4 1.6 copy_dynamic-update-slice_fusion.2
  1223.0 1.4 add_select_fusion.6
  1225.6 268.1 %cosine_convert_fusion.2 = (bf16[64,128,2048]{2,1,0:T(8,128)(2,1)}, bf16[64,128,2048]{2,1,0:T(8,128)(2,1)}) fusion(s32[128,2048]{1,0:T(8,128)S(1)} %add_select_fusion.6, s32[64]{0:T(128)S(1)} %iota_add_fusion.3), kind=kLoop, calls=%fused_computation.14.clone.1 | loop fusion | flops 268435456 | bytes 68157696 | tf_op jit(solution)/shard_map/convert
  1495.8 22.4 fusion.176
  1518.2 1.6 copy_dynamic-update-slice_fusion.2
  1519.8 1.4 add_select_fusion.6
  1522.5 268.1 %cosine_convert_fusion.2 = (bf16[64,128,2048]{2,1,0:T(8,128)(2,1)}, bf16[64,128,2048]{2,1,0:T(8,128)(2,1)}) fusion(s32[128,2048]{1,0:T(8,128)S(1)} %add_select_fusion.6, s32[64]{0:T(128)S(1)} %iota_add_fusion.3), kind=kLoop, calls=%fused_computation.14.clone.1 | loop fusion | flops 268435456 | bytes 68157696 | tf_op jit(solution)/shard_map/convert
  1792.7 22.4 fusion.176
  1815.1 1.6 copy_dynamic-update-slice_fusion.2
  1816.7 1.4 add_select_fusion.6
  1819.3 268.1 %cosine_convert_fusion.2 = (bf16[64,128,2048]{2,1,0:T(8,128)(2,1)}, bf16[64,128,2048]{2,1,0:T(8,128)(2,1)}) fusion(s32[128,2048]{1,0:T(8,128)S(1)} %add_select_fusion.6, s32[64]{0:T(128)S(1)} %iota_add_fusion.3), kind=kLoop, calls=%fused_computation.14.clone.1 | loop fusion | flops 268435456 | bytes 68157696 | tf_op jit(solution)/shard_map/convert
  2089.5 22.4 fusion.176
  2112.0 1.6 copy_dynamic-update-slice_fusion.2
  2113.5 1.4 add_select_fusion.6
  2116.2 268.1 %cosine_convert_fusion.2 = (bf16[64,128,2048]{2,1,0:T(8,128)(2,1)}, bf16[64,128,2048]{2,1,0:T(8,128)(2,1)}) fusion(s32[128,2048]{1,0:T(8,128)S(1)} %add_select_fusion.6, s32[64]{0:T(128)S(1)} %iota_add_fusion.3), kind=kLoop, calls=%fused_computation.14.clone.1 | loop fusion | flops 268435456 | bytes 68157696 | tf_op jit(solution)/shard_map/convert
  2386.4 22.4 fusion.176
  2408.8 1.6 copy_dynamic-update-slice_fusion.2
  2410.6 143.9 %reduce-scatter.2.cloned.1.call-done = f32[8,64,2,512]{3,1,0,2:T(8,128)} async-done(((f32[8,64,2,2048]{3,1,0,2:T(8,128)}), f32[8,64,2,512]{3,1,0,2:T(8,128)}) %reduce-scatter.2.cloned.1.call-update) | async-done | bytes 2097168 | tf_op jit(solution)/shard_map/reduce_scatter | solution.py:96
  2554.5 1.8 broadcast_multiply_fusion
  2556.3 1.7 collective-permute-start.1
  2558.2 1.8 collective-permute-done.1
  2560.0 2.7 collective-permute-done
  2562.7 3.7 fusion.30
  (90 shorter events, 7.1 us)
Async XLA Ops:
  6.5 1.0 copy-start
  18.4 14.9 all-to-all-start
  23.5 2531.0 %reduce-scatter.2.cloned.1.call-start = ((), (), s32[]{:S(2)}) async-start(), calls=%async_computation.2 | async-start | bytes 10485760 | tf_op jit(solution)/shard_map/reduce_scatter | solution.py:96
  35.4 2375.1 %copy-start.2 = (s32[8]{0:T(128)S(1)}, s32[8]{0:T(128)}, u32[]{:S(2)}) copy-start(s32[8]{0:T(128)} %param.9) | copy-start | bytes 100
  2410.5 156.0 %copy-start.1 = (f32[1,128,512]{2,1,0:T(8,128)S(1)}, f32[1,128,512]{2,1,0:T(8,128)}, u32[]{:S(2)}) copy-start(f32[1,128,512]{2,1,0:T(8,128)} %param.6) | copy-start | bytes 786436
  2556.3 3.6 collective-permute-start.1
  2558.1 4.6 collective-permute-start
Sparse Core Ops, SparseCore 0:
  2410.6 143.8 reduce-scatter.1
where the time goes:
time: 2570 us
  other arithmetic  2160 us (84%)
  matrix products  191 us (7%)
  waiting for transfers between devices  157 us (6%)
    another operation x8, other arithmetic  2140 us
    dot_general x8, matrix products, one_band(): jnp.einsum('krc,kcm->krm', operand, ramp_table, preferred_element_type=jn...  179 us
    reduce_scatter x1, waiting for transfers between devices, shards(): lax.psum_scatter(partial_terms, 'chan', scatter_dimension=3, tiled=True)  144 us
  transfers between devices with their start and end apart: 4, of which 4 were waited for; matrix products, arithmetic and copies ran while one was open for 0% of the time, Pallas kernels for 0%

commit v1 on v0

v1 whole, which is shorter than its diff:
```python
import math

import jax
import jax.numpy as jnp
import numpy as np
from jax import lax
from jax.experimental import pallas as pl
from jax.experimental.pallas import tpu as pltpu
from jax.sharding import PartitionSpec as P

CHANNELS = 512
GROUPS = 64
BANDS = 8
HALF = 4
FLOOR_VALUE = 0.5


def phasor(steps, total):
    shift = (total // 2).bit_length() - 1
    turned = steps + total // 4
    quadrant = turned >> shift
    rest = (turned & (total // 2 - 1)) - total // 4
    x = rest.astype(jnp.float32) * (math.pi / total)
    x2 = x * x
    sine = x + x * x2 * (-1 / 6 + x2 * (1 / 120 + x2 * (-1 / 5040 + x2 * (1 / 362880))))
    cosine = 1.0 + x2 * (-0.5 + x2 * (1 / 24 + x2 * (-1 / 720 + x2 * (1 / 40320))))
    odd = (quadrant & 1) == 1
    c = jnp.where(odd, sine, cosine)
    s = jnp.where(odd, cosine, sine)
    c = jnp.where(((quadrant + 1) & 2) == 2, -c, c)
    s = jnp.where((quadrant & 2) == 2, -s, s)
    return c, s


def times(a, b):
    return a[0] * b[0] - a[1] * b[1], a[0] * b[1] + a[1] * b[0]


def search(total, length, shard, scal, lhs, dm, out, centers, offset, step, powers):
    window = shard + 2 * HALF
    pairs = window // 2
    first = scal[0] * shard
    tile = dm.shape[1]
    group = lax.broadcasted_iota(jnp.int32, (GROUPS, tile), 0)
    remain = GROUPS - group
    sweep = (2048 * remain * remain) // (GROUPS * GROUPS)
    delay = (dm[...] * sweep) >> 10
    double = 2 * (first - HALF) + window - 1
    c, s = phasor(delay, total)
    offset[0], offset[1] = c, s
    c, s = phasor(2 * delay, total)
    step[0], step[1] = c, s
    wide = phasor(2 * length * delay, total)
    center = phasor(double * delay, total)
    for band in range(BANDS):
        centers[band, 0], centers[band, 1] = center
        if band < BANDS - 1:
            center = times(center, wide)

    def one_pair(j, carry):
        cb, sb = offset[0], offset[1]
        for duo in range(BANDS // 2):
            coefs = lhs[j, duo]
            high = coefs.astype(jnp.bfloat16).astype(jnp.float32)
            rows = jnp.concatenate([high, coefs - high], axis=0).astype(jnp.bfloat16)
            for part in range(2):
                band = 2 * duo + part
                ca, sa = centers[band, 0], centers[band, 1]
                table = jnp.concatenate(
                    [
                        (ca * cb).astype(jnp.bfloat16),
                        (sa * sb).astype(jnp.bfloat16),
                        (sa * cb).astype(jnp.bfloat16),
                        (ca * sb).astype(jnp.bfloat16),
                    ],
                    axis=0,
                )
                both = jnp.dot(rows, table, preferred_element_type=jnp.float32)
                value = both[:8] + both[8:]
                square = value * value
                at = 4 * part
                power = (square[at : at + 2] + square[at + 2 : at + 4]) * (1.0 / CHANNELS)
                powers[band, pl.ds(pairs + j, 1)] = power[0:1]
                powers[band, pl.ds(pairs - 1 - j, 1)] = power[1:2]
        offset[0], offset[1] = times((cb, sb), (step[0], step[1]))
        return carry

    lax.fori_loop(0, pairs, one_pair, 0)

    row = lax.broadcasted_iota(jnp.int32, (shard, tile), 0)
    for band in range(BANDS):
        half_width = scal[1 + band]
        at = row + (band * length + first)
        total_sum = jnp.zeros((shard, tile), jnp.float32)
        counted = jnp.zeros((shard, tile), jnp.float32)
        for move in range(-HALF, HALF + 1):
            near = at + move
            inside = (near >= 0) & (near < BANDS * length) & (abs(move) <= half_width)
            total_sum += jnp.where(inside, powers[band, HALF + move : HALF + move + shard], 0.0)
            counted += jnp.where(inside, 1.0, 0.0)
        middle = powers[band, HALF : HALF + shard]
        out[band] = middle / jnp.maximum(total_sum / counted, FLOOR_VALUE)


def shards(samples, groups, dm_delay, widths):
    highest = lax.Precision.HIGHEST
    phases = lax.axis_size("bins")
    chans = lax.axis_size("chan")
    phase = lax.axis_index("bins")
    chan = lax.axis_index("chan")
    local, length = samples.shape[1:]
    shard = length // phases
    total = length * phases
    window = shard + 2 * HALF
    pairs = window // 2
    share = GROUPS // chans

    mine = lax.dynamic_slice_in_dim(groups, chan * local, local)
    chosen = (mine[None, :] == jnp.arange(GROUPS, dtype=jnp.int32)[:, None]).astype(jnp.float32)
    series = jnp.dot(chosen, samples[0], precision=highest)
    series = lax.psum_scatter(series, "chan", scatter_dimension=0, tiled=True)

    bins = (np.arange(phases) * shard)[:, None] + np.arange(window)[None, :] - HALF
    turn = (np.arange(length)[:, None] * (bins.reshape(-1) % length)[None, :]) % length
    angle = turn * (2 * np.pi / length)
    scale = total**-0.5
    first = np.concatenate([np.cos(angle), -np.sin(angle)], axis=1) * scale
    freq = jnp.dot(series, jnp.asarray(first, jnp.float32), precision=highest)
    freq = freq.reshape(share, 2, phases, window)
    twist = (phase * jnp.asarray(bins, jnp.int32)).astype(jnp.float32) * (2 * math.pi / total)
    tc, ts = jnp.cos(twist), jnp.sin(twist)
    real = freq[:, 0] * tc + freq[:, 1] * ts
    imag = freq[:, 1] * tc - freq[:, 0] * ts
    blocks = jnp.stack([real, imag], axis=0).transpose(2, 0, 1, 3)
    blocks = jnp.broadcast_to(blocks[:, None], (phases, chans, 2, share, window))
    blocks = blocks.reshape(phases * chans, 2, share, window)
    got = lax.all_to_all(blocks, ("bins", "chan"), split_axis=0, concat_axis=0, tiled=True)
    got = got.reshape(phases, chans, 2, share, window)
    second = (np.arange(phases)[:, None] * np.arange(BANDS)[None, :]) % phases * (2 * np.pi / phases)
    c2, s2 = jnp.asarray(np.cos(second), jnp.float32), jnp.asarray(np.sin(second), jnp.float32)
    if phases <= 16:
        weave = lambda x, t: sum(x[i][None] * t[i][:, None, None, None] for i in range(phases))
    else:
        weave = lambda x, t: jnp.einsum("izgw,ib->bzgw", x, t, precision=highest)
    real = weave(got[:, :, 0], c2) + weave(got[:, :, 1], s2)
    imag = weave(got[:, :, 1], c2) - weave(got[:, :, 0], s2)
    real = real.reshape(BANDS, GROUPS, window)
    imag = imag.reshape(BANDS, GROUPS, window)

    rp, ip = real[:, :, pairs:], imag[:, :, pairs:]
    rm, im = real[:, :, :pairs][:, :, ::-1], imag[:, :, :pairs][:, :, ::-1]
    lhs = jnp.stack(
        [
            jnp.stack([rp, -rp, -ip, -ip]),
            jnp.stack([rm, rm, -im, im]),
            jnp.stack([ip, -ip, rp, rp]),
            jnp.stack([im, im, rm, -rm]),
        ]
    )
    lhs = lhs.transpose(4, 2, 0, 1, 3).reshape(pairs, BANDS // 2, 8, 4 * GROUPS)

    trials = dm_delay.shape[0] // chans
    tile = min(256, trials)
    dm = lax.dynamic_slice_in_dim(dm_delay, chan * trials, trials)[None, :]
    scal = jnp.concatenate([jnp.reshape(phase, (1,)), widths])
    kernel = lambda *refs: search(total, length, shard, *refs)
    return pl.pallas_call(
        kernel,
        grid=(trials // tile,),
        in_specs=[
            pl.BlockSpec(memory_space=pltpu.SMEM),
            pl.BlockSpec(lhs.shape, lambda i: (0, 0, 0, 0)),
            pl.BlockSpec((1, tile), lambda i: (0, i)),
        ],
        out_specs=pl.BlockSpec((BANDS, shard, tile), lambda i: (0, 0, i)),
        out_shape=jax.ShapeDtypeStruct((BANDS, shard, trials), jnp.float32),
        scratch_shapes=[
            pltpu.VMEM((BANDS, 2, GROUPS, tile), jnp.float32),
            pltpu.VMEM((2, GROUPS, tile), jnp.float32),
            pltpu.VMEM((2, GROUPS, tile), jnp.float32),
            pltpu.VMEM((BANDS, window, tile), jnp.float32),
        ],
        compiler_params=pltpu.CompilerParams(vmem_limit_bytes=40 * 1024 * 1024),
        cost_estimate=pl.CostEstimate(
            flops=2 * pairs * BANDS * 16 * 256 * trials, bytes_accessed=4 << 20, transcendentals=0
        ),
        name="search",
    )(scal, lhs, dm)


def solution(mesh):
    in_specs = (P("bins", "chan", None), P(), P(), P())
    out_specs = P(None, "bins", "chan")
    return jax.shard_map(shards, mesh=mesh, in_specs=in_specs, out_specs=out_specs, check_vma=False)
```

time: 2570 us -> 95 us (0.04)
  other arithmetic: 2160 us -> 4.54 us
  matrix products: 191 us -> 3.81 us
  waiting for transfers between devices: 157 us -> 35.9 us
    another operation x16 -> x7, other arithmetic: 2140 us -> 0.88 us  [the longest x3 0.78 us: shards(): jnp.stack([jnp.stack([rp, -rp, -ip, -ip]), jnp.stack([rm, rm, -im, im]),...]
    dot_general x14 -> x2, matrix products: 191 us -> 3.81 us  [the longest x1 2.91 us: shards(): freq = jnp.dot(series, jnp.asarray(first, jnp.float32), precision=highest)]
    reduce_scatter x1, waiting for transfers between devices: 144 us -> 22.3 us  [shards(): series = lax.psum_scatter(series, 'chan', scatter_dimension=0, tiled=True)]
  transfers between devices with their start and end apart: 4 -> 2, of which waited for: 4 -> 2; matrix products, arithmetic and copies ran while one was open for 0% -> 2% of each run, Pallas kernels for 0% -> 0%
where the time goes in v1:
time: 95 us; the launch traced here: 94 us
  waiting for transfers between devices  35.9 us (38%)
  Pallas kernels  25 us (26%)
  between operations  13.9 us (15%)
  local copies, waits for them, and re-layouts  8.1 us (9%)
  other arithmetic  4.54 us (5%)
  matrix products  3.81 us (4%)
  starting transfers between devices  2.79 us (3%)
    pallas_call x1, Pallas kernels, shards(): pl.pallas_call(kernel, grid=(trials // tile,), in_specs=[pl.BlockSpec(mem...  25 us
    reduce_scatter x1, waiting for transfers between devices, shards(): series = lax.psum_scatter(series, 'chan', scatter_dimension=0, tiled=True)  22.3 us
    all_to_all x1, waiting for transfers between devices, shards(): lax.all_to_all(blocks, ('bins', 'chan'), split_axis=0, concat_axis=0, til...  13.5 us
    dot_general x1, matrix products, shards(): freq = jnp.dot(series, jnp.asarray(first, jnp.float32), precision=highest)  2.91 us
    all_to_all x1, starting transfers between devices, shards(): lax.all_to_all(blocks, ('bins', 'chan'), split_axis=0, concat_axis=0, til...  2.78 us
    reshape x1, local copies, waits for them, and re-layouts, shards(): lhs = lhs.transpose(4, 2, 0, 1, 3).reshape(pairs, BANDS // 2, 8, 4 * GROUPS)  2.62 us
    transpose x1, other arithmetic, shards(): lhs = lhs.transpose(4, 2, 0, 1, 3).reshape(pairs, BANDS // 2, 8, 4 * GROUPS)  2.07 us
  transfers between devices with their start and end apart: 2, of which 2 were waited for; matrix products, arithmetic and copies ran while one was open for 2% of the time, Pallas kernels for 0%

profile of v1, /device:TPU:0, one launch (start us, length us, event | category | flops | bytes accessed | tf_op | source)
XLA Modules:
  0.0 94.0 jit_solution(5468395965738685323)
XLA Ops:
  6.5 0.8 dynamic_slice.6
  7.3 0.2 copy-done
  7.5 0.9 fusion
  8.4 0.0 reduce-scatter.2.cloned.1.call-update
  8.4 0.7 fusion.4
  9.2 22.3 %reduce-scatter.2.cloned.1.call-done = f32[16,512]{1,0:T(8,128)} async-done(((f32[64,512]{1,0:T(8,128)}), f32[16,512]{1,0:T(8,128)}) %reduce-scatter.2.cloned.1.call-update) | async-done | bytes 32784 | tf_op jit(solution)/shard_map/reduce_scatter | solution.py:121
  31.5 2.9 %fusion.6 = f32[16,1152]{1,0:T(8,128)S(1)} fusion(f32[16,512]{1,0:T(8,128)} %reduce-scatter.2.cloned.1.call-done, f32[512,1152]{1,0:T(8,128)} %constant.27.clone), kind=kOutput, calls=%fused_computation.31 | convolution fusion | flops 113246208 | bytes 2465792 | tf_op jit(solution)/shard_map/dot_general | solution.py:128
  34.4 0.1 reshape.180
  34.6 0.0 copy-start.1
  34.6 0.0 copy-start.2
  34.6 0.0 copy-start.4
  34.6 0.0 copy-start.5
  34.7 0.0 copy-start.6
  34.7 0.0 copy-start.7
  34.7 0.0 copy-start.8
  34.8 0.9 broadcast_in_dim.4
  35.7 2.8 %all-to-all-start = ((f32[32,2,16,72]{3,2,1,0:T(8,128)}), f32[32,2,16,72]{3,2,1,0:T(8,128)S(1)}, u32[]{:S(2)}, u32[]{:S(2)}) async-start(f32[32,2,16,72]{3,2,1,0:T(8,128)} %bitcast.5), calls=%async_computation.1 | async-start | bytes 1048576 | tf_op jit(solution)/shard_map/all_to_all | solution.py:137
  38.5 0.8 dynamic_slice.7
  39.2 0.1 pad_add_fusion.refs_0_
  39.3 13.5 %all-to-all-done = f32[32,2,16,72]{3,2,1,0:T(8,128)S(1)} async-done(((f32[32,2,16,72]{3,2,1,0:T(8,128)}), f32[32,2,16,72]{3,2,1,0:T(8,128)S(1)}, u32[]{:S(2)}, u32[]{:S(2)}) %all-to-all-start) | async-done | bytes 294944 | tf_op jit(solution)/shard_map/all_to_all | solution.py:137
  52.9 0.1 copy.36
  53.0 0.1 copy.20
  53.1 0.1 copy.21
  53.1 0.1 copy.22
  53.2 0.1 copy.23
  53.3 0.1 copy.24
  53.4 0.1 copy.25
  53.5 0.1 copy.26
  53.6 0.1 copy.28
  53.7 0.1 copy.29
  53.8 0.1 copy.30
  53.8 0.1 copy.31
  53.9 0.1 copy.32
  54.0 0.1 copy.33
  54.1 0.1 copy.34
  54.2 0.1 copy.35
  54.4 0.4 add_subtract_fusion
  54.9 0.1 copy.27
  55.0 0.1 copy.19
  55.0 0.4 add_add_fusion
  55.5 0.4 copy.41
  55.9 0.1 maximum_bitcast_fusion.1
  56.0 0.4 copy.40
  56.4 0.4 copy.42
  56.8 0.7 maximum_bitcast_fusion.4
  57.5 2.1 %maximum_bitcast_fusion = f32[36,8,4,4,64]{4,3,2,1,0:T(4,128)} fusion(f32[1,4,8,64,36]{3,1,0,2,4:T(4,128)S(1)} %maximum_bitcast_fusion.4, f32[1,4,8,64,36]{3,1,0,2,4:T(4,128)S(1)} %copy.42, f32[1,4,8,64,36]{3,1,0,2,4:T(4,128)S(1)} %copy.41, f32[1,4,8,64,36]{3,1,0,2,4:T(4,128)S(1)} %copy.40), kind=kLoop, calls=%fused_computation | loop fusion | flops 884736 | bytes 2359296 | tf_op jit(solution)/shard_map/transpose | solution.py:160
  59.5 2.6 %reshape.183.refs_1_ = f32[36,4,8,256]{3,2,1,0:T(8,128)S(1)} reshape(f32[36,8,4,4,64]{4,3,2,1,0:T(4,128)} %maximum_bitcast_fusion) | data formatting | bytes 2359296 | tf_op jit(solution)/shard_map/reshape | solution.py:160
  62.2 25.0 %search.1 = f32[8,64,512]{2,1,0:T(8,128)} custom-call(s32[9]{0:T(128)S(1)} %pad_add_fusion.refs_0_, f32[36,4,8,256]{3,2,1,0:T(8,128)S(1)} %reshape.183.refs_1_, s32[1,512]{1,0:T(1,128)S(1)} %bitcast.73), custom_call_target="tpu_custom_call" | custom-call | flops 1207959552 | bytes 4194304 | tf_op jit(solution)/shard_map/search/pallas_call | solution.py:167
  (37 shorter events, 0.3 us)
Async XLA Ops:
  6.5 1.0 %copy-start = (f32[1,128,512]{2,1,0:T(8,128)S(1)}, f32[1,128,512]{2,1,0:T(8,128)}, u32[]{:S(2)}) copy-start(f32[1,128,512]{2,1,0:T(8,128)} %param.8) | copy-start | bytes 786436
  6.5 25.0 %reduce-scatter.2.cloned.1.call-start = ((), (), s32[]{:S(2)}) async-start(), calls=%async_computation.2 | async-start | bytes 163840 | tf_op jit(solution)/shard_map/reduce_scatter | solution.py:121
  9.2 30.1 %copy-start.15 = (s32[8]{0:T(128)S(1)}, s32[8]{0:T(128)}, u32[]{:S(2)}) copy-start(s32[8]{0:T(128)} %param.11) | copy-start | bytes 100
  34.6 19.7 %copy-start.1 = (f32[8]{0:T(128)S(1)}, f32[8]{0:T(128)}, u32[]{:S(2)}) copy-start(f32[8]{0:T(128)} %constant.35) | copy-start | bytes 100
  34.6 19.7 %copy-start.2 = (f32[8]{0:T(128)S(1)}, f32[8]{0:T(128)}, u32[]{:S(2)}) copy-start(f32[8]{0:T(128)} %constant.37) | copy-start | bytes 100
  34.6 19.7 %copy-start.3 = (f32[8]{0:T(128)S(1)}, f32[8]{0:T(128)}, u32[]{:S(2)}) copy-start(f32[8]{0:T(128)} %constant.39) | copy-start | bytes 100
  34.6 19.7 %copy-start.4 = (f32[8]{0:T(128)S(1)}, f32[8]{0:T(128)}, u32[]{:S(2)}) copy-start(f32[8]{0:T(128)} %constant.41) | copy-start | bytes 100
  34.6 19.7 %copy-start.5 = (f32[8]{0:T(128)S(1)}, f32[8]{0:T(128)}, u32[]{:S(2)}) copy-start(f32[8]{0:T(128)} %constant.43) | copy-start | bytes 100
  34.7 19.7 %copy-start.6 = (f32[8]{0:T(128)S(1)}, f32[8]{0:T(128)}, u32[]{:S(2)}) copy-start(f32[8]{0:T(128)} %constant.45) | copy-start | bytes 100
  34.7 19.7 %copy-start.7 = (f32[8]{0:T(128)S(1)}, f32[8]{0:T(128)}, u32[]{:S(2)}) copy-start(f32[8]{0:T(128)} %constant.47) | copy-start | bytes 100
  34.7 19.7 %copy-start.8 = (f32[8]{0:T(128)S(1)}, f32[8]{0:T(128)}, u32[]{:S(2)}) copy-start(f32[8]{0:T(128)} %constant.51) | copy-start | bytes 100
  34.7 19.7 %copy-start.9 = (f32[8]{0:T(128)S(1)}, f32[8]{0:T(128)}, u32[]{:S(2)}) copy-start(f32[8]{0:T(128)} %constant.53) | copy-start | bytes 100
  34.7 19.7 %copy-start.10 = (f32[8]{0:T(128)S(1)}, f32[8]{0:T(128)}, u32[]{:S(2)}) copy-start(f32[8]{0:T(128)} %constant.55) | copy-start | bytes 100
  34.7 19.7 %copy-start.11 = (f32[8]{0:T(128)S(1)}, f32[8]{0:T(128)}, u32[]{:S(2)}) copy-start(f32[8]{0:T(128)} %constant.57) | copy-start | bytes 100
  34.7 19.7 %copy-start.12 = (f32[8]{0:T(128)S(1)}, f32[8]{0:T(128)}, u32[]{:S(2)}) copy-start(f32[8]{0:T(128)} %constant.59) | copy-start | bytes 100
  34.7 19.7 %copy-start.13 = (f32[8]{0:T(128)S(1)}, f32[8]{0:T(128)}, u32[]{:S(2)}) copy-start(f32[8]{0:T(128)} %constant.61) | copy-start | bytes 100
  34.8 19.6 %copy-start.14 = (f32[8]{0:T(128)S(1)}, f32[8]{0:T(128)}, u32[]{:S(2)}) copy-start(f32[8]{0:T(128)} %constant.63) | copy-start | bytes 100
  35.7 17.2 %all-to-all-start = ((f32[32,2,16,72]{3,2,1,0:T(8,128)}), f32[32,2,16,72]{3,2,1,0:T(8,128)S(1)}, u32[]{:S(2)}, u32[]{:S(2)}) async-start(f32[32,2,16,72]{3,2,1,0:T(8,128)} %bitcast.5), calls=%async_computation.1 | async-start | bytes 1048576 | tf_op jit(solution)/shard_map/all_to_all | solution.py:137
Sparse Core Ops, SparseCore 0:
  9.6 21.8 reduce-scatter.1

commit v2 on v1

--- a/solution.py
+++ b/solution.py
@@ -13,6 +13,8 @@
 BANDS = 8
 HALF = 4
 FLOOR_VALUE = 0.5
+TILE = 256
+MESH = pl.DeviceIdType.MESH
 
 
 def phasor(steps, total):
@@ -36,15 +38,120 @@
     return a[0] * b[0] - a[1] * b[1], a[0] * b[1] + a[1] * b[0]
 
 
-def search(total, length, shard, scal, lhs, dm, out, centers, offset, step, powers):
+def front(phases, chans, shard, samples, groups, table_hbm, out, table, parts, gathered, near, blocks, arrived,
+          load_sem, send_sem, recv_sem):
+    phase, chan = lax.axis_index("bins"), lax.axis_index("chan")
+    window = shard + 2 * HALF
+    total = phases * samples.shape[2]
+    share = GROUPS // chans
+    load = pltpu.make_async_copy(table_hbm, table, load_sem)
+    load.start()
+    barrier = pltpu.get_barrier_semaphore()
+    for off in range(1, chans):
+        pl.semaphore_signal(barrier, 1, device_id=(phase, lax.rem(chan + off, chans)), device_id_type=MESH)
+    for off in range(1, phases):
+        pl.semaphore_signal(barrier, 1, device_id=(lax.rem(phase + off, phases), chan), device_id_type=MESH)
+
+    mine = groups[pl.ds(chan, 1), :]
+    chosen = jnp.where(
+        mine == lax.broadcasted_iota(jnp.int32, (GROUPS, groups.shape[1]), 0), 1.0, 0.0
+    )
+    series = jnp.dot(
+        chosen, samples[0], precision=lax.Precision.HIGHEST, preferred_element_type=jnp.float32
+    )
+    parts[...] = series.reshape(parts.shape)
+    pl.semaphore_wait(barrier, chans + phases - 2)
+
+    copies = []
+    for off in range(1, chans):
+        peer = lax.rem(chan + off, chans)
+        copy = pltpu.make_async_remote_copy(
+            src_ref=parts.at[peer],
+            dst_ref=near.at[off - 1],
+            send_sem=send_sem.at[off - 1],
+            recv_sem=recv_sem.at[off - 1],
+            device_id=(phase, peer),
+            device_id_type=MESH,
+        )
+        copy.start()
+        copies.append(copy)
+    shape = (phases, window, GROUPS)
+    place = lax.broadcasted_iota(jnp.int32, shape, 0) * shard + lax.broadcasted_iota(jnp.int32, shape, 1) - HALF
+    tc, ts = phasor((2 * phase * place) & (2 * total - 1), total)
+    own = parts[chan]
+    for copy in copies:
+        copy.wait()
+    for off in range(1, chans):
+        own = own + near[off - 1]
+    gathered[pl.ds(chan, 1)] = own[None]
+
+    copies = []
+    for off in range(1, chans):
+        copy = pltpu.make_async_remote_copy(
+            src_ref=gathered.at[chan],
+            dst_ref=gathered.at[chan],
+            send_sem=send_sem.at[chans - 2 + off],
+            recv_sem=recv_sem.at[chans - 2 + off],
+            device_id=(phase, lax.rem(chan + off, chans)),
+            device_id_type=MESH,
+        )
+        copy.start()
+        copies.append(copy)
+    load.wait()
+    for copy in copies:
+        copy.wait()
+
+    whole = gathered[...].reshape(GROUPS, samples.shape[2])
+    high = whole.astype(jnp.bfloat16)
+    low = (whole - high.astype(jnp.float32)).astype(jnp.bfloat16)
+    dims = (((1,), (1,)), ((), ()))
+    freq = (
+        lax.dot_general(table[0], high, dims, preferred_element_type=jnp.float32)
+        + lax.dot_general(table[0], low, dims, preferred_element_type=jnp.float32)
+        + lax.dot_general(table[1], high, dims, preferred_element_type=jnp.float32)
+    )
+    real = freq[: phases * window].reshape(shape)
+    imag = freq[phases * window :].reshape(shape)
+    blocks[...] = jnp.concatenate([real * tc + imag * ts, imag * tc - real * ts], axis=2)
+    copies = []
+    for off in range(1, phases):
+        peer = lax.rem(phase + off, phases)
+        slot = 2 * (chans - 1) + off - 1
+        copy = pltpu.make_async_remote_copy(
+            src_ref=blocks.at[peer],
+            dst_ref=arrived.at[phase],
+            send_sem=send_sem.at[slot],
+            recv_sem=recv_sem.at[slot],
+            device_id=(peer, chan),
+            device_id_type=MESH,
+        )
+        copy.start()
+        copies.append(copy)
+    arrived[pl.ds(phase, 1)] = blocks[pl.ds(phase, 1)]
+    for copy in copies:
+        copy.wait()
+    lane = lax.broadcasted_iota(jnp.int32, (window, 2 * GROUPS), 1)
+    sign = jnp.where(lane < GROUPS, 1.0, -1.0)
+    for band in range(BANDS):
+        straight = jnp.zeros((window, 2 * GROUPS), jnp.float32)
+        crossed = jnp.zeros((window, 2 * GROUPS), jnp.float32)
+        for source in range(phases):
+            angle = 2 * math.pi * (source * band % phases) / phases
+            block = arrived[source]
+            straight += block * math.cos(angle)
+            crossed += block * math.sin(angle)
+        out[band] = straight + pltpu.roll(crossed, GROUPS, 1) * sign
+
+
+def search(total, length, shard, widths, spectra, dm, out, centers, offset, step, powers):
     window = shard + 2 * HALF
     pairs = window // 2
-    first = scal[0] * shard
+    first = lax.axis_index("bins") * shard
     tile = dm.shape[1]
     group = lax.broadcasted_iota(jnp.int32, (GROUPS, tile), 0)
     remain = GROUPS - group
     sweep = (2048 * remain * remain) // (GROUPS * GROUPS)
-    delay = (dm[...] * sweep) >> 10
+    delay = (dm[pl.ds(lax.axis_index("chan"), 1), :] * sweep) >> 10
     double = 2 * (first - HALF) + window - 1
     c, s = phasor(delay, total)
     offset[0], offset[1] = c, s
@@ -57,10 +164,28 @@
         if band < BANDS - 1:
             center = times(center, wide)
 
+    tile8 = (8, 2 * GROUPS)
+    row8 = lax.broadcasted_iota(jnp.int32, tile8, 0)
+    left = lax.broadcasted_iota(jnp.int32, tile8, 1) < GROUPS
+    real_row = (row8 & 1) == 0
+    plus_row = (row8 & 2) == 0
+    low_part = row8 < 4
+    sign_first = jnp.where(real_row & ~left, -1.0, 1.0)
+    sign_second = jnp.where(plus_row & (real_row | left) | ~plus_row & ~real_row & ~left, -1.0, 1.0)
+
     def one_pair(j, carry):
         cb, sb = offset[0], offset[1]
         for duo in range(BANDS // 2):
-            coefs = lhs[j, duo]
+            row = [
+                jnp.broadcast_to(spectra[2 * duo + part, pl.ds(at, 1), :], tile8)
+                for part in range(2)
+                for at in (pairs + j, pairs - 1 - j)
+            ]
+            value = jnp.where(
+                low_part, jnp.where(plus_row, row[0], row[1]), jnp.where(plus_row, row[2], row[3])
+            )
+            value = jnp.where(real_row, value, pltpu.roll(value, GROUPS, 1))
+            coefs = jnp.concatenate([value * sign_first, value * sign_second], axis=1)
             high = coefs.astype(jnp.bfloat16).astype(jnp.float32)
             rows = jnp.concatenate([high, coefs - high], axis=0).astype(jnp.bfloat16)
             for part in range(2):
@@ -69,19 +194,18 @@
                 table = jnp.concatenate(
                     [
                         (ca * cb).astype(jnp.bfloat16),
+                        (sa * cb).astype(jnp.bfloat16),
                         (sa * sb).astype(jnp.bfloat16),
-                        (sa * cb).astype(jnp.bfloat16),
                         (ca * sb).astype(jnp.bfloat16),
                     ],
                     axis=0,
                 )
                 both = jnp.dot(rows, table, preferred_element_type=jnp.float32)
-                value = both[:8] + both[8:]
-                square = value * value
+                total_rows = both[:8] + both[8:]
+                square = total_rows * total_rows * (1.0 / CHANNELS)
                 at = 4 * part
-                power = (square[at : at + 2] + square[at + 2 : at + 4]) * (1.0 / CHANNELS)
-                powers[band, pl.ds(pairs + j, 1)] = power[0:1]
-                powers[band, pl.ds(pairs - 1 - j, 1)] = power[1:2]
+                powers[band, pl.ds(pairs + j, 1)] = square[at : at + 1] + square[at + 1 : at + 2]
+                powers[band, pl.ds(pairs - 1 - j, 1)] = square[at + 2 : at + 3] + square[at + 3 : at + 4]
         offset[0], offset[1] = times((cb, sb), (step[0], step[1]))
         return carry
 
@@ -89,7 +213,7 @@
 
     row = lax.broadcasted_iota(jnp.int32, (shard, tile), 0)
     for band in range(BANDS):
-        half_width = scal[1 + band]
+        half_width = widths[band]
         at = row + (band * length + first)
         total_sum = jnp.zeros((shard, tile), jnp.float32)
         counted = jnp.zeros((shard, tile), jnp.float32)
@@ -102,25 +226,62 @@
         out[band] = middle / jnp.maximum(total_sum / counted, FLOOR_VALUE)
 
 
-def shards(samples, groups, dm_delay, widths):
+def block_bins(phases, shard):
+    return (np.arange(phases) * shard)[:, None] + np.arange(shard + 2 * HALF)[None, :] - HALF
+
+
+def spectra_by_kernel(samples, groups, phases, chans, shard):
+    local, length = samples.shape[1:]
+    window = shard + 2 * HALF
+    bins = block_bins(phases, shard)
+    turn = ((bins.reshape(-1) % length)[:, None] * np.arange(length)[None, :]) % length
+    angle = turn * (2 * np.pi / length)
+    scale = (length * phases) ** -0.5
+    exact = (np.concatenate([np.cos(angle), -np.sin(angle)], axis=0) * scale).astype(np.float32)
+    high = exact.astype(jnp.bfloat16)
+    low = (exact - high.astype(np.float32)).astype(jnp.bfloat16)
+    table = jnp.asarray(np.stack([high, low]))
+    share = GROUPS // chans
+    copies = 2 * (chans - 1) + phases - 1
+    vmem = pl.BlockSpec(memory_space=pltpu.VMEM)
+    return pl.pallas_call(
+        lambda *refs: front(phases, chans, shard, *refs),
+        in_specs=[vmem, vmem, pl.BlockSpec(memory_space=pl.ANY)],
+        out_specs=vmem,
+        out_shape=jax.ShapeDtypeStruct((BANDS, window, 2 * GROUPS), jnp.float32),
+        scratch_shapes=[
+            pltpu.VMEM(table.shape, jnp.bfloat16),
+            pltpu.VMEM((chans, share, length), jnp.float32),
+            pltpu.VMEM((chans, share, length), jnp.float32),
+            pltpu.VMEM((chans - 1, share, length), jnp.float32),
+            pltpu.VMEM((phases, window, 2 * GROUPS), jnp.float32),
+            pltpu.VMEM((phases, window, 2 * GROUPS), jnp.float32),
+            pltpu.SemaphoreType.DMA,
+            pltpu.SemaphoreType.DMA((copies,)),
+            pltpu.SemaphoreType.DMA((copies,)),
+        ],
+        compiler_params=pltpu.CompilerParams(
+            collective_id=0, has_side_effects=True, vmem_limit_bytes=32 * 1024 * 1024
+        ),
+        cost_estimate=pl.CostEstimate(flops=1 << 28, bytes_accessed=4 << 20, transcendentals=0),
+        name="front",
+    )(samples, groups.reshape(chans, local), table)
+
+
+def spectra_by_collectives(samples, groups, phases, chans, shard):
     highest = lax.Precision.HIGHEST
-    phases = lax.axis_size("bins")
-    chans = lax.axis_size("chan")
     phase = lax.axis_index("bins")
     chan = lax.axis_index("chan")
     local, length = samples.shape[1:]
-    shard = length // phases
     total = length * phases
     window = shard + 2 * HALF
-    pairs = window // 2
     share = GROUPS // chans
-
     mine = lax.dynamic_slice_in_dim(groups, chan * local, local)
     chosen = (mine[None, :] == jnp.arange(GROUPS, dtype=jnp.int32)[:, None]).astype(jnp.float32)
     series = jnp.dot(chosen, samples[0], precision=highest)
     series = lax.psum_scatter(series, "chan", scatter_dimension=0, tiled=True)
 
-    bins = (np.arange(phases) * shard)[:, None] + np.arange(window)[None, :] - HALF
+    bins = block_bins(phases, shard)
     turn = (np.arange(length)[:, None] * (bins.reshape(-1) % length)[None, :]) % length
     angle = turn * (2 * np.pi / length)
     scale = total**-0.5
@@ -138,39 +299,31 @@
     got = got.reshape(phases, chans, 2, share, window)
     second = (np.arange(phases)[:, None] * np.arange(BANDS)[None, :]) % phases * (2 * np.pi / phases)
     c2, s2 = jnp.asarray(np.cos(second), jnp.float32), jnp.asarray(np.sin(second), jnp.float32)
-    if phases <= 16:
-        weave = lambda x, t: sum(x[i][None] * t[i][:, None, None, None] for i in range(phases))
-    else:
-        weave = lambda x, t: jnp.einsum("izgw,ib->bzgw", x, t, precision=highest)
+    weave = lambda x, t: jnp.einsum("izgw,ib->bwzg", x, t, precision=highest)
     real = weave(got[:, :, 0], c2) + weave(got[:, :, 1], s2)
     imag = weave(got[:, :, 1], c2) - weave(got[:, :, 0], s2)
-    real = real.reshape(BANDS, GROUPS, window)
-    imag = imag.reshape(BANDS, GROUPS, window)
-
-    rp, ip = real[:, :, pairs:], imag[:, :, pairs:]
-    rm, im = real[:, :, :pairs][:, :, ::-1], imag[:, :, :pairs][:, :, ::-1]
-    lhs = jnp.stack(
-        [
-            jnp.stack([rp, -rp, -ip, -ip]),
-            jnp.stack([rm, rm, -im, im]),
-            jnp.stack([ip, -ip, rp, rp]),
-            jnp.stack([im, im, rm, -rm]),
-        ]
-    )
-    lhs = lhs.transpose(4, 2, 0, 1, 3).reshape(pairs, BANDS // 2, 8, 4 * GROUPS)
-
+    return jnp.stack([real, imag], axis=2).reshape(BANDS, window, 2 * GROUPS)
+
+
+def shards(samples, groups, dm_delay, widths):
+    phases = lax.axis_size("bins")
+    chans = lax.axis_size("chan")
+    length = samples.shape[2]
+    shard = length // phases
+    total = length * phases
+    window = shard + 2 * HALF
+    pairs = window // 2
+    make = spectra_by_kernel if window % 8 == 0 else spectra_by_collectives
+    spectra = make(samples, groups, phases, chans, shard)
     trials = dm_delay.shape[0] // chans
-    tile = min(256, trials)
-    dm = lax.dynamic_slice_in_dim(dm_delay, chan * trials, trials)[None, :]
-    scal = jnp.concatenate([jnp.reshape(phase, (1,)), widths])
-    kernel = lambda *refs: search(total, length, shard, *refs)
+    tile = min(TILE, trials)
     return pl.pallas_call(
-        kernel,
+        lambda *refs: search(total, length, shard, *refs),
         grid=(trials // tile,),
         in_specs=[
             pl.BlockSpec(memory_space=pltpu.SMEM),
-            pl.BlockSpec(lhs.shape, lambda i: (0, 0, 0, 0)),
-            pl.BlockSpec((1, tile), lambda i: (0, i)),
+            pl.BlockSpec(spectra.shape, lambda i: (0, 0, 0)),
+            pl.BlockSpec((chans, tile), lambda i: (0, i)),
         ],
         out_specs=pl.BlockSpec((BANDS, shard, tile), lambda i: (0, 0, i)),
         out_shape=jax.ShapeDtypeStruct((BANDS, shard, trials), jnp.float32),
@@ -185,7 +338,7 @@
             flops=2 * pairs * BANDS * 16 * 256 * trials, bytes_accessed=4 << 20, transcendentals=0
         ),
         name="search",
-    )(scal, lhs, dm)
+    )(widths, spectra, dm_delay.reshape(chans, trials))
 
 
 def solution(mesh):

time: 95 us -> 51.1 us (0.54)
  waiting for transfers between devices: 35.9 us -> 0 us
  Pallas kernels: 25 us -> 46.8 us
  between operations: 13.9 us -> 0.02 us
  other arithmetic: 4.54 us -> 0 us
  local copies, waits for them, and re-layouts: 8.1 us -> 4.02 us
  matrix products: 3.81 us -> 0 us
  starting transfers between devices: 2.79 us -> 0 us
    reduce_scatter x1 -> x0, waiting for transfers between devices: 22.3 us -> none  [shards(): series = lax.psum_scatter(series, 'chan', scatter_dimension=0, tiled=True)]
    pallas_call x1 -> x2, Pallas kernels: 25 us -> 46.8 us  [the longest x1 27 us: shards(): pl.pallas_call(lambda *refs: search(total, length, shard, *refs), grid=(t...]
    all_to_all x1 -> x0, waiting for transfers between devices: 13.5 us -> none  [shards(): lax.all_to_all(blocks, ('bins', 'chan'), split_axis=0, concat_axis=0, til...]
    dot_general x2 -> x0, matrix products: 3.81 us -> none  [the longest x1 2.91 us: shards(): freq = jnp.dot(series, jnp.asarray(first, jnp.float32), precision=highest)]
    unnamed x32 -> x8, local copies, waits for them, and re-layouts: 0.27 us -> 3.3 us
    all_to_all x1 -> x0, starting transfers between devices: 2.78 us -> none  [shards(): lax.all_to_all(blocks, ('bins', 'chan'), split_axis=0, concat_axis=0, til...]
    transpose x2 -> x0, other arithmetic: 2.08 us -> none  [the longest x1 2.07 us: shards(): lhs = lhs.transpose(4, 2, 0, 1, 3).reshape(pairs, BANDS // 2, 8, 4 * GROUPS)]
    reshape x2 -> x1, local copies, waits for them, and re-layouts: 2.75 us -> 0.72 us  [shards(): dm_delay.reshape(chans, trials)]
  transfers between devices with their start and end apart: 2 -> 0, of which waited for: 2 -> 0; matrix products, arithmetic and copies ran while one was open for 2% -> 0% of each run, Pallas kernels for 0% -> 0%
where the time goes in v2:
time: 51.1 us; the launch traced here: 50.9 us
  Pallas kernels  46.8 us (92%)
  local copies, waits for them, and re-layouts  4.02 us (8%)
    pallas_call x1, Pallas kernels, shards(): pl.pallas_call(lambda *refs: search(total, length, shard, *refs), grid=(t...  27 us
    pallas_call x1, Pallas kernels, spectra_by_kernel(): pl.pallas_call(lambda *refs: front(phases, chans, shard, *refs), in_specs...  19.8 us
    unnamed x8, local copies, waits for them, and re-layouts  3.3 us

profile of v2, /device:TPU:0, one launch (start us, length us, event | category | flops | bytes accessed | tf_op | source)
XLA Modules:
  0.0 50.9 jit_solution(14746454020030929105)
XLA Ops:
  0.0 0.0 copy-start.3
  0.0 0.7 %reshape.7.refs_2_ = s32[4,512]{1,0:T(4,128)S(1)} reshape(s32[2048]{0:T(1024)} %param.7) | data formatting | bytes 16384 | tf_op jit(solution)/shard_map/reshape | solution.py:341
  0.7 0.0 copy-start
  0.7 1.7 %copy-done = bf16[2,1152,512]{2,1,0:T(8,128)(2,1)S(1)} copy-done((bf16[2,1152,512]{2,1,0:T(8,128)(2,1)S(1)}, bf16[2,1152,512]{2,1,0:T(8,128)(2,1)}, u32[]{:S(2)}) %copy-start) | copy-done | bytes 2359320
  2.4 0.0 copy-start.1
  2.4 0.9 %copy-done.1 = f32[1,128,512]{2,1,0:T(8,128)S(1)} copy-done((f32[1,128,512]{2,1,0:T(8,128)S(1)}, f32[1,128,512]{2,1,0:T(8,128)}, u32[]{:S(2)}) %copy-start.1) | copy-done | bytes 262168
  3.3 0.0 copy-start.2
  3.3 0.7 %copy-done.2 = s32[512]{0:T(512)S(1)} copy-done((s32[512]{0:T(512)S(1)}, s32[512]{0:T(512)}, u32[]{:S(2)}) %copy-start.2) | copy-done | bytes 2072
  4.0 19.8 %front.1.refs_1_ = f32[8,72,128]{2,1,0:T(8,128)S(1)} custom-call(f32[1,128,512]{2,1,0:T(8,128)S(1)} %copy-done.1, s32[4,128]{1,0:T(4,128)S(1)} %bitcast.1, bf16[2,1152,512]{2,1,0:T(8,128)(2,1)S(1)} %copy-done), custom_call_target="tpu_custom_call" | custom-call | flops 268435456 | bytes 4194304 | tf_op jit(solution)/shard_map/front/pallas_call | solution.py:247
  23.9 0.0 copy-done.3
  23.9 27.0 %search.1 = f32[8,64,512]{2,1,0:T(8,128)} custom-call(s32[8]{0:T(128)S(1)} %copy-done.3, f32[8,72,128]{2,1,0:T(8,128)S(1)} %front.1.refs_1_, s32[4,512]{1,0:T(4,128)S(1)} %reshape.7.refs_2_), custom_call_target="tpu_custom_call" | custom-call | flops 1207959552 | bytes 4194304 | tf_op jit(solution)/shard_map/search/pallas_call | solution.py:320
Async XLA Ops:
  0.0 23.9 %copy-start.3 = (s32[8]{0:T(128)S(1)}, s32[8]{0:T(128)}, u32[]{:S(2)}) copy-start(s32[8]{0:T(128)} %refs_0_.3) | copy-start | bytes 100
  0.7 1.7 %copy-start = (bf16[2,1152,512]{2,1,0:T(8,128)(2,1)S(1)}, bf16[2,1152,512]{2,1,0:T(8,128)(2,1)}, u32[]{:S(2)}) copy-start(bf16[2,1152,512]{2,1,0:T(8,128)(2,1)} %constant.2.clone.refs_2_) | copy-start | bytes 7077892
  2.4 0.9 %copy-start.1 = (f32[1,128,512]{2,1,0:T(8,128)S(1)}, f32[1,128,512]{2,1,0:T(8,128)}, u32[]{:S(2)}) copy-start(f32[1,128,512]{2,1,0:T(8,128)} %refs_0_.2) | copy-start | bytes 786436
  3.3 0.7 %copy-start.2 = (s32[512]{0:T(512)S(1)}, s32[512]{0:T(512)}, u32[]{:S(2)}) copy-start(s32[512]{0:T(512)} %param.6) | copy-start | bytes 6148

commit v3 on v2

--- a/solution.py
+++ b/solution.py
@@ -13,7 +13,7 @@
 BANDS = 8
 HALF = 4
 FLOOR_VALUE = 0.5
-TILE = 256
+TILE = 512
 MESH = pl.DeviceIdType.MESH
 
 
@@ -211,19 +211,32 @@
 
     lax.fori_loop(0, pairs, one_pair, 0)
 
-    row = lax.broadcasted_iota(jnp.int32, (shard, tile), 0)
+    @pl.when(first == 0)
+    def _():
+        powers[0, 0:HALF] = jnp.zeros((HALF, tile), jnp.float32)
+
+    @pl.when(first + shard == length)
+    def _():
+        powers[BANDS - 1, HALF + shard : window] = jnp.zeros((HALF, tile), jnp.float32)
+
+    row = lax.broadcasted_iota(jnp.int32, (shard, 128), 0)
     for band in range(BANDS):
         half_width = widths[band]
         at = row + (band * length + first)
-        total_sum = jnp.zeros((shard, tile), jnp.float32)
-        counted = jnp.zeros((shard, tile), jnp.float32)
-        for move in range(-HALF, HALF + 1):
-            near = at + move
-            inside = (near >= 0) & (near < BANDS * length) & (abs(move) <= half_width)
-            total_sum += jnp.where(inside, powers[band, HALF + move : HALF + move + shard], 0.0)
-            counted += jnp.where(inside, 1.0, 0.0)
-        middle = powers[band, HALF : HALF + shard]
-        out[band] = middle / jnp.maximum(total_sum / counted, FLOOR_VALUE)
+        low_end = jnp.maximum(at - half_width, 0)
+        high_end = jnp.minimum(at + half_width, BANDS * length - 1)
+        part = 1.0 / (high_end - low_end + 1).astype(jnp.float32)
+        weight = [jnp.where(move <= half_width, 1.0, 0.0) for move in range(HALF + 1)]
+        for column in range(0, tile, 128):
+            lanes = slice(column, column + 128)
+            middle = powers[band, HALF : HALF + shard, lanes]
+            total_sum = middle
+            for move in range(1, HALF + 1):
+                total_sum += weight[move] * (
+                    powers[band, HALF - move : HALF - move + shard, lanes]
+                    + powers[band, HALF + move : HALF + move + shard, lanes]
+                )
+            out[band, :, lanes] = middle / jnp.maximum(total_sum * part, FLOOR_VALUE)
 
 
 def block_bins(phases, shard):
@@ -261,7 +274,7 @@
             pltpu.SemaphoreType.DMA((copies,)),
         ],
         compiler_params=pltpu.CompilerParams(
-            collective_id=0, has_side_effects=True, vmem_limit_bytes=32 * 1024 * 1024
+            collective_id=0, has_side_effects=True, vmem_limit_bytes=60 * 1024 * 1024
         ),
         cost_estimate=pl.CostEstimate(flops=1 << 28, bytes_accessed=4 << 20, transcendentals=0),
         name="front",
@@ -333,7 +346,7 @@
             pltpu.VMEM((2, GROUPS, tile), jnp.float32),
             pltpu.VMEM((BANDS, window, tile), jnp.float32),
         ],
-        compiler_params=pltpu.CompilerParams(vmem_limit_bytes=40 * 1024 * 1024),
+        compiler_params=pltpu.CompilerParams(vmem_limit_bytes=60 * 1024 * 1024),
         cost_estimate=pl.CostEstimate(
             flops=2 * pairs * BANDS * 16 * 256 * trials, bytes_accessed=4 << 20, transcendentals=0
         ),

time: 51.1 us -> 43.6 us (0.85)
  Pallas kernels: 46.8 us -> 42 us
  local copies, waits for them, and re-layouts: 4.02 us -> 1.31 us
    pallas_call x1, Pallas kernels: 27 us -> 20.8 us  [shards(): pl.pallas_call(lambda *refs: search(total, length, shard, *refs), grid=(t...]
    unnamed x8 -> x0, local copies, waits for them, and re-layouts: 3.3 us -> none
    pallas_call x1, Pallas kernels: 19.8 us -> 21.3 us  [spectra_by_kernel(): pl.pallas_call(lambda *refs: front(phases, chans, shard, *refs), in_specs...]
    reshape x1, local copies, waits for them, and re-layouts: 0.72 us -> 1.31 us  [shards(): dm_delay.reshape(chans, trials)]
where the time goes in v3:
time: 43.6 us; the launch traced here: 43.4 us
  Pallas kernels  42 us (96%)
  local copies, waits for them, and re-layouts  1.31 us (3%)
    pallas_call x1, Pallas kernels, spectra_by_kernel(): pl.pallas_call(lambda *refs: front(phases, chans, shard, *refs), in_specs...  21.3 us
    pallas_call x1, Pallas kernels, shards(): pl.pallas_call(lambda *refs: search(total, length, shard, *refs), grid=(t...  20.8 us
    reshape x1, local copies, waits for them, and re-layouts, shards(): dm_delay.reshape(chans, trials)  1.31 us

profile of v3, /device:TPU:0, one launch (start us, length us, event | category | flops | bytes accessed | tf_op | source)
XLA Modules:
  0.0 43.4 jit_solution(14150001626550458791)
XLA Ops:
  0.0 1.3 %reshape.7.refs_2_ = s32[4,512]{1,0:T(4,128)} reshape(s32[2048]{0:T(1024)} %param.7) | data formatting | bytes 16384 | tf_op jit(solution)/shard_map/reshape | solution.py:354
  1.3 21.3 %front.1.refs_1_ = f32[8,72,128]{2,1,0:T(8,128)} custom-call(f32[1,128,512]{2,1,0:T(8,128)} %refs_0_.2, s32[4,128]{1,0:T(4,128)} %bitcast.1, bf16[2,1152,512]{2,1,0:T(8,128)(2,1)} %constant.2.clone.refs_2_), custom_call_target="tpu_custom_call" | custom-call | flops 268435456 | bytes 4194304 | tf_op jit(solution)/shard_map/front/pallas_call | solution.py:260
  22.6 20.8 %search.1 = f32[8,64,512]{2,1,0:T(8,128)} custom-call(s32[8]{0:T(128)} %refs_0_.3, f32[8,72,128]{2,1,0:T(8,128)} %front.1.refs_1_, s32[4,512]{1,0:T(4,128)} %reshape.7.refs_2_), custom_call_target="tpu_custom_call" | custom-call | flops 1207959552 | bytes 4194304 | tf_op jit(solution)/shard_map/search/pallas_call | solution.py:333

commit v4 on v3

--- a/solution.py
+++ b/solution.py
@@ -147,11 +147,13 @@
     window = shard + 2 * HALF
     pairs = window // 2
     first = lax.axis_index("bins") * shard
-    tile = dm.shape[1]
+    tile = out.shape[2]
     group = lax.broadcasted_iota(jnp.int32, (GROUPS, tile), 0)
     remain = GROUPS - group
     sweep = (2048 * remain * remain) // (GROUPS * GROUPS)
-    delay = (dm[pl.ds(lax.axis_index("chan"), 1), :] * sweep) >> 10
+    place = lax.axis_index("chan") * pl.num_programs(0) + pl.program_id(0)
+    trial = dm[:, pl.ds(pl.multiple_of(place * tile, tile), tile)]
+    delay = (trial * sweep) >> 10
     double = 2 * (first - HALF) + window - 1
     c, s = phasor(delay, total)
     offset[0], offset[1] = c, s
@@ -336,7 +338,7 @@
         in_specs=[
             pl.BlockSpec(memory_space=pltpu.SMEM),
             pl.BlockSpec(spectra.shape, lambda i: (0, 0, 0)),
-            pl.BlockSpec((chans, tile), lambda i: (0, i)),
+            pl.BlockSpec((1, chans * trials), lambda i: (0, 0)),
         ],
         out_specs=pl.BlockSpec((BANDS, shard, tile), lambda i: (0, 0, i)),
         out_shape=jax.ShapeDtypeStruct((BANDS, shard, trials), jnp.float32),
@@ -351,7 +353,7 @@
             flops=2 * pairs * BANDS * 16 * 256 * trials, bytes_accessed=4 << 20, transcendentals=0
         ),
         name="search",
-    )(widths, spectra, dm_delay.reshape(chans, trials))
+    )(widths, spectra, dm_delay[None])
 
 
 def solution(mesh):

time: 43.6 us -> 42.2 us (0.968)
  local copies, waits for them, and re-layouts: 1.31 us -> 0 us
    reshape x1 -> x0, local copies, waits for them, and re-layouts: 1.31 us -> none  [shards(): dm_delay.reshape(chans, trials)]
where the time goes in v4:
time: 42.2 us; the launch traced here: 42.1 us
  Pallas kernels  42 us (100%)
    pallas_call x1, Pallas kernels, spectra_by_kernel(): pl.pallas_call(lambda *refs: front(phases, chans, shard, *refs), in_specs...  21.3 us
    pallas_call x1, Pallas kernels, shards(): pl.pallas_call(lambda *refs: search(total, length, shard, *refs), grid=(t...  20.8 us

profile of v4, /device:TPU:0, one launch (start us, length us, event | category | flops | bytes accessed | tf_op | source)
XLA Modules:
  0.0 42.1 jit_solution(8942509483953740921)
XLA Ops:
  0.0 21.3 %front.1.refs_1_ = f32[8,72,128]{2,1,0:T(8,128)} custom-call(f32[1,128,512]{2,1,0:T(8,128)} %refs_0_.2, s32[4,128]{1,0:T(4,128)} %bitcast.2, bf16[2,1152,512]{2,1,0:T(8,128)(2,1)} %constant.2.clone.refs_2_), custom_call_target="tpu_custom_call" | custom-call | flops 268435456 | bytes 4194304 | tf_op jit(solution)/shard_map/front/pallas_call | solution.py:262
  21.3 20.8 %search.1 = f32[8,64,512]{2,1,0:T(8,128)} custom-call(s32[8]{0:T(128)} %refs_0_.3, f32[8,72,128]{2,1,0:T(8,128)} %front.1.refs_1_, s32[1,2048]{1,0:T(1,128)} %bitcast.3), custom_call_target="tpu_custom_call" | custom-call | flops 1207959552 | bytes 4194304 | tf_op jit(solution)/shard_map/search/pallas_call | solution.py:335
